TPU v7x, 512 devices: a whole 4x4x16 slice. The times are simulated.
512 devices in a mesh: cell: 32 (over x, y, core), gene: 16 (over z).
Axes of the slice: x: 4, y: 4, z: 16, core: 2. Of those that a mesh axis runs over, the one named last changes fastest.
Arguments:
- counts: int32 [8192, 8192], P('cell', 'gene'), may hold values from 0 to 83, as said below
- prior_basis: float32 [8192, 128], P('gene'), may hold values from -0.0625 to 0.0625
- prior_values: float32 [128], replicated, may hold values from 0.3 to 1.5
Outputs:
- loadings: float32 [8192, 128], P('gene')
- scores: float32 [8192, 128], P('cell')
Inputs may be any that keep to these rules, and one draw needn't show every extreme that they name: `counts`: every cell has a nonzero count in at least one gene.
All inputs are finite; a program needn't handle non-finite values.
Results may differ from a plain program's by a relative error of at most 0.0003.
Values sent between devices are 32-bit elements; how exact they have to be, the bound alone decides.
A program may use at most 64 MiB of HBM per device.

v0:
```python
import jax
import jax.numpy as jnp
from jax import lax
from jax.sharding import PartitionSpec as P

ITERS = 3


scale_factor = 10000.0
highest = lax.Precision.HIGHEST


def merged_2(value, axis, combine):
    everything = jax.tree.map(lambda part: lax.all_gather(part, axis), value)
    leading = jax.tree.map(lambda part: part[0], everything)

    def turn(k, so_far):
        return combine(so_far, jax.tree.map(lambda part: part[k], everything))

    return lax.fori_loop(1, lax.axis_size(axis), turn, leading)


def matmul(left, right):
    return jnp.dot(left, right, precision=highest, preferred_element_type=jnp.float32)


def inner(left, right):
    return lax.dot_general(
        left, right, (((0,), (0,)), ((), ())), precision=highest, preferred_element_type=jnp.float32
    )


def combine(first, second):
    count_a, mean_a, proj_a, image_a = first
    count_b, mean_b, proj_b, image_b = second
    count = count_a + count_b
    share = count_b / count
    delta = mean_b - mean_a
    delta_proj = proj_b - proj_a
    image = image_a + image_b + count_a * share * delta[:, None] * delta_proj[None, :]
    return (count, mean_a + share * delta, proj_a + share * delta_proj, image)


def orthonormal(image, lower_gram):
    lower = jnp.linalg.cholesky(lower_gram)
    return lax.linalg.triangular_solve(lower, image, left_side=False, lower=True, transpose_a=True)


def per_device(counts, prior_basis, prior_values):
    expression = counts.astype(jnp.float32)
    library = lax.psum(jnp.sum(expression, axis=1), "gene")
    expression = jnp.log1p(scale_factor * expression / library[:, None])
    rows = expression.shape[0]
    gene_rows = expression.shape[1]
    groups = lax.axis_size("cell")
    total = jnp.float32(rows * groups)
    weights = prior_values * prior_values
    width = jnp.sqrt(jnp.float32(gene_rows * lax.axis_size("gene")))
    basis = prior_basis
    mean_all = jnp.zeros((gene_rows,), jnp.float32)
    for step in range(ITERS):
        projected, correlation = lax.psum(
            (matmul(expression, basis), inner(prior_basis, basis)), "gene"
        )
        mixing = weights[:, None] * correlation
        mean_local = jnp.mean(expression, axis=0)
        proj_local = jnp.mean(projected, axis=0)
        local_image = inner(expression, projected - proj_local[None, :])
        merged = merged_2((jnp.float32(rows), mean_local, proj_local, local_image), "cell", combine)
        mean_all = merged[1]
        image = merged[3] / total + matmul(prior_basis, mixing)
        gram = lax.psum(inner(image, image), "gene")
        basis = orthonormal(image, gram)
    cell_part, mean_part = lax.psum(
        (matmul(expression, basis), matmul(mean_all[None, :], basis)[0]), "gene"
    )
    return (width * basis, cell_part - mean_part[None, :])


def solution(mesh):
    return jax.shard_map(
        per_device,
        mesh=mesh,
        in_specs=(P("cell", "gene"), P("gene", None), P()),
        out_specs=(P("gene", None), P("cell", None)),
        check_vma=False,
    )
```

profile of v0, /device:TPU:1, one launch (start us, length us, event | category | flops | bytes accessed | tf_op | source)
XLA Modules:
  0.0 1597.4 jit_solution(8255247612747475517)
XLA Ops:
  8.4 30.3 %psum.84 = f32[256]{0:T(256)S(1)} all-reduce(f32[256]{0:T(256)S(1)} %convert_reduce_fusion), channel_id=1, replica_groups=mesh['cell'=32,'gene'=16] {'gene'}, use_global_device_ids=true, to_apply=%region_1.0 | all-reduce | flops 256 | bytes 2048 | tf_op jit(solution)/shard_map/psum | solution.py:51
  38.8 1.3 fusion.46
  42.7 128.2 %all-reduce.24.cloned.1.call-done = (f32[256,128]{1,0:T(8,128)}, f32[128,128]{1,0:T(8,128)}) async-done(((f32[256,128]{1,0:T(8,128)}, f32[128,128]{1,0:T(8,128)}), (f32[256,128]{1,0:T(8,128)}, f32[128,128]{1,0:T(8,128)})) %all-reduce.24.cloned.1.call-update) | async-done | bytes 196624 | tf_op jit(solution)/shard_map/psum | solution.py:62
  171.9 2.6 fusion.16
  174.6 34.8 %all-gather.7 = f32[32,1,512]{2,1,0:T(1,128)S(1)} all-gather(f32[1,1,512]{2,1,0:T(1,128)S(1)} %bitcast.176), channel_id=2, replica_groups=mesh['cell'=32,'gene'=16] {'cell'}, dimensions={0}, use_global_device_ids=true | all-gather | bytes 67584 | tf_op jit(solution)/shard_map/all_gather | solution.py:14
  211.4 62.6 %all-reduce = f32[32]{0:T(128)S(1)} all-reduce(f32[32]{0:T(128)S(1)} %dynamic-update-slice.2), channel_id=1, replica_groups=mesh['cell'=32,'gene'=16] {'cell'}, use_global_device_ids=true, to_apply=%add | all-reduce | flops 32 | bytes 256
  274.8 20.4 %all-gather.8 = f32[32,1,128]{2,1,0:T(1,128)S(1)} all-gather(f32[1,1,128]{2,1,0:T(1,128)S(1)} %get-tuple-element.752), channel_id=3, replica_groups=mesh['cell'=32,'gene'=16] {'cell'}, dimensions={0}, use_global_device_ids=true | all-gather | bytes 16896 | tf_op jit(solution)/shard_map/all_gather | solution.py:14
  296.2 95.4 %while.63 = (s32[]{:T(128)}, f32[]{:T(128)}, f32[512]{0:T(512)S(1)}, f32[128]{0:T(128)S(1)}, f32[512,128]{1,0:T(8,128)S(1)}, /*index=5*/f32[32]{0:T(128)S(1)}, f...) while((s32[]{:T(128)}, f32[]{:T(128)}, ...), condition=%wide.region_6.0_spmd, body=%wide.region_5.0_spmd.sunk | while | flops 199048 | bytes 803567 | solution.py:20
  391.7 1.3 fusion.11
  394.3 117.7 %all-reduce.12.cloned.1.call-done = f32[128,128]{0,1:T(8,128)} async-done(((f32[128,128]{0,1:T(8,128)}), f32[128,128]{0,1:T(8,128)}) %all-reduce.12.cloned.1.call-update) | async-done | bytes 65552 | tf_op jit(solution)/shard_map/psum | solution.py:72
  513.8 11.7 cholesky.59
  526.8 9.8 custom-call.7
  539.6 132.2 %all-reduce.22.cloned.1.call-done = (f32[256,128]{1,0:T(8,128)}, f32[128,128]{1,0:T(8,128)}) async-done(((f32[256,128]{1,0:T(8,128)}, f32[128,128]{1,0:T(8,128)}), (f32[256,128]{1,0:T(8,128)}, f32[128,128]{1,0:T(8,128)})) %all-reduce.22.cloned.1.call-update) | async-done | bytes 196624 | tf_op jit(solution)/shard_map/psum | solution.py:62
  672.8 2.6 fusion.14
  675.5 32.1 %all-gather.9 = f32[32,1,128]{2,1,0:T(1,128)S(1)} all-gather(f32[1,1,128]{2,1,0:T(1,128)S(1)} %get-tuple-element.750), channel_id=5, replica_groups=mesh['cell'=32,'gene'=16] {'cell'}, dimensions={0}, use_global_device_ids=true | all-gather | bytes 16896 | tf_op jit(solution)/shard_map/all_gather | solution.py:14
  707.6 42.9 %all-gather.17.cloned.1.call-done = f32[16384,128]{1,0:T(8,128)} async-done(((f32[512,128]{1,0:T(8,128)}), f32[16384,128]{1,0:T(8,128)}) %all-gather.17.cloned.1.call-update) | async-done | bytes 8388624 | tf_op jit(solution)/shard_map/all_gather | solution.py:14
  751.4 95.4 %while.64 = (s32[]{:T(128)}, f32[]{:T(128)}, f32[512]{0:T(512)S(1)}, f32[128]{0:T(128)S(1)}, f32[512,128]{1,0:T(8,128)S(1)}, /*index=5*/f32[32]{0:T(128)S(1)}, f...) while((s32[]{:T(128)}, f32[]{:T(128)}, ...), condition=%wide.region_14.17_spmd, body=%wide.region_13.16_spmd.sunk | while | flops 199048 | bytes 803567 | solution.py:20
  849.6 121.5 %all-reduce.14.cloned.1.call-done = f32[128,128]{0,1:T(8,128)} async-done(((f32[128,128]{0,1:T(8,128)}), f32[128,128]{0,1:T(8,128)}) %all-reduce.14.cloned.1.call-update) | async-done | bytes 65552 | tf_op jit(solution)/shard_map/psum | solution.py:72
  972.9 11.7 cholesky.70
  986.0 9.8 custom-call.8
  998.8 132.2 %all-reduce.20.cloned.1.call-done = (f32[256,128]{1,0:T(8,128)}, f32[128,128]{1,0:T(8,128)}) async-done(((f32[256,128]{1,0:T(8,128)}, f32[128,128]{1,0:T(8,128)}), (f32[256,128]{1,0:T(8,128)}, f32[128,128]{1,0:T(8,128)})) %all-reduce.20.cloned.1.call-update) | async-done | bytes 196624 | tf_op jit(solution)/shard_map/psum | solution.py:62
  1131.9 2.6 fusion.12
  1134.7 32.1 %all-gather.10 = f32[32,1,128]{2,1,0:T(1,128)S(1)} all-gather(f32[1,1,128]{2,1,0:T(1,128)S(1)} %get-tuple-element.748), channel_id=7, replica_groups=mesh['cell'=32,'gene'=16] {'cell'}, dimensions={0}, use_global_device_ids=true | all-gather | bytes 16896 | tf_op jit(solution)/shard_map/all_gather | solution.py:14
  1166.7 43.0 %all-gather.19.cloned.1.call-done = f32[16384,128]{1,0:T(8,128)} async-done(((f32[512,128]{1,0:T(8,128)}), f32[16384,128]{1,0:T(8,128)}) %all-gather.19.cloned.1.call-update) | async-done | bytes 8388624 | tf_op jit(solution)/shard_map/all_gather | solution.py:14
  1210.7 95.5 %while.65 = (s32[]{:T(128)}, f32[]{:T(128)}, f32[512]{0:T(512)S(1)}, f32[128]{0:T(128)S(1)}, f32[512,128]{1,0:T(8,128)S(1)}, /*index=5*/f32[32]{0:T(128)S(1)}, f...) while((s32[]{:T(128)}, f32[]{:T(128)}, ...), condition=%wide.region_20.23_spmd, body=%wide.region_19.22_spmd.sunk | while | flops 199048 | bytes 803567 | solution.py:20
  1306.3 1.3 fusion.9
  1309.0 121.5 %all-reduce.16.cloned.1.call-done = f32[128,128]{0,1:T(8,128)} async-done(((f32[128,128]{0,1:T(8,128)}), f32[128,128]{0,1:T(8,128)}) %all-reduce.16.cloned.1.call-update) | async-done | bytes 65552 | tf_op jit(solution)/shard_map/psum | solution.py:72
  1432.3 11.7 cholesky.81
  1445.3 9.8 custom-call.9
  1457.9 21.4 %psum.95 = f32[128]{0:T(128)S(1)} all-reduce(f32[128]{0:T(128)S(1)} %convolution_bitcast_fusion.8), channel_id=1, replica_groups=mesh['cell'=32,'gene'=16] {'gene'}, use_global_device_ids=true, to_apply=%region_24.27 | all-reduce | flops 128 | bytes 1024 | tf_op jit(solution)/shard_map/psum | solution.py:74
  1479.4 109.7 %all-reduce.18.cloned.1.call-done = f32[256,128]{1,0:T(8,128)} async-done(((f32[256,128]{1,0:T(8,128)}), f32[256,128]{1,0:T(8,128)}) %all-reduce.18.cloned.1.call-update) | async-done | bytes 131088 | tf_op jit(solution)/shard_map/psum | solution.py:74
  1589.0 1.6 broadcast_subtract_fusion
  (544 shorter events, 197.5 us)
Async XLA Ops:
  7.2 32.9 %copy-start = (f32[512,128]{1,0:T(8,128)S(1)}, f32[512,128]{1,0:T(8,128)}, u32[]{:S(2)}) copy-start(f32[512,128]{1,0:T(8,128)} %param.13) | copy-start | bytes 786436
  7.2 163.7 %all-reduce.24.cloned.1.call-start = ((), (), s32[]{:S(2)}) async-start(), calls=%async_computation.9 | async-start | bytes 393216 | tf_op jit(solution)/shard_map/psum | solution.py:62
  42.6 252.6 %all-gather.15.cloned.1.call-start = ((), (), s32[]{:S(2)}) async-start(), calls=%async_computation.4 | async-start | bytes 8650752 | tf_op jit(solution)/shard_map/all_gather | solution.py:14
  174.5 337.5 %all-reduce.12.cloned.1.call-start = ((), (), s32[]{:S(2)}) async-start(), calls=%async_computation | async-start | bytes 131072 | tf_op jit(solution)/shard_map/psum | solution.py:72
  394.1 277.8 %all-reduce.22.cloned.1.call-start = ((), (), s32[]{:S(2)}) async-start(), calls=%async_computation.8 | async-start | bytes 393216 | tf_op jit(solution)/shard_map/psum | solution.py:62
  539.6 210.9 %all-gather.17.cloned.1.call-start = ((), (), s32[]{:S(2)}) async-start(), calls=%async_computation.5 | async-start | bytes 8650752 | tf_op jit(solution)/shard_map/all_gather | solution.py:14
  675.4 295.7 %all-reduce.14.cloned.1.call-start = ((), (), s32[]{:S(2)}) async-start(), calls=%async_computation.1 | async-start | bytes 131072 | tf_op jit(solution)/shard_map/psum | solution.py:72
  849.3 281.6 %all-reduce.20.cloned.1.call-start = ((), (), s32[]{:S(2)}) async-start(), calls=%async_computation.7 | async-start | bytes 393216 | tf_op jit(solution)/shard_map/psum | solution.py:62
  998.7 211.1 %all-gather.19.cloned.1.call-start = ((), (), s32[]{:S(2)}) async-start(), calls=%async_computation.6 | async-start | bytes 8650752 | tf_op jit(solution)/shard_map/all_gather | solution.py:14
  1134.6 295.9 %all-reduce.16.cloned.1.call-start = ((), (), s32[]{:S(2)}) async-start(), calls=%async_computation.2 | async-start | bytes 131072 | tf_op jit(solution)/shard_map/psum | solution.py:72
  1308.7 280.3 %all-reduce.18.cloned.1.call-start = ((), (), s32[]{:S(2)}) async-start(), calls=%async_computation.3 | async-start | bytes 262144 | tf_op jit(solution)/shard_map/psum | solution.py:74
Sparse Core Ops, SparseCore 0:
  42.7 128.1 all-reduce.23
  175.1 74.7 all-gather.14
  394.2 117.7 all-reduce.11
  539.7 132.1 all-reduce.21
  675.9 74.5 all-gather.16
  849.5 121.6 all-reduce.13
  998.8 132.1 all-reduce.19
  1135.2 74.5 all-gather.18
  1308.8 121.6 all-reduce.15
  1457.0 132.0 all-reduce.17
where the time goes:
time: 1610 us; the launch traced here: 1600 us
  waiting for transfers between devices  949 us (59%)
  blocking collectives  234 us (15%)
  other arithmetic  184 us (11%)
  loops' own time  125 us (8%)
  local copies, waits for them, and re-layouts  64.7 us (4%)
  matrix products  25 us (2%)
    psum x3, waiting for transfers between devices, per_device(): lax.psum((matmul(expression, basis), inner(prior_basis, basis)), 'gene')  393 us
    psum x3, waiting for transfers between devices, per_device(): gram = lax.psum(inner(image, image), 'gene')  361 us
    another operation x3, loops' own time, merged_2(): return lax.fori_loop(1, lax.axis_size(axis), turn, leading)  125 us
    all_gather x4, blocking collectives, merged_2(): everything = jax.tree.map(lambda part: lax.all_gather(part, axis), value)  119 us
    psum x1, waiting for transfers between devices, per_device(): lax.psum((matmul(expression, basis), matmul(mean_all[None, :], basis)[0])...  110 us
    add x93, other arithmetic, combine(): image_a + image_b + count_a * share * delta[:, None] * delta_proj[None, :]  102 us
    all_gather x3, waiting for transfers between devices, merged_2(): everything = jax.tree.map(lambda part: lax.all_gather(part, axis), value)  85.9 us
    unnamed x1, blocking collectives  62.6 us
  transfers between devices with their start and end apart: 10, of which 9 were waited for; matrix products, arithmetic and copies ran while one was open for 0% of the time, Pallas kernels for 0%

commit v1 on v0

v1 whole, which is shorter than its diff:
```python
import functools

import jax
import jax.numpy as jnp
from jax import lax
from jax.experimental import pallas as pl
from jax.experimental.pallas import tpu as pltpu
from jax.sharding import PartitionSpec as P

ITERS = 3
SCALE = 10000.0
HIGHEST = lax.Precision.HIGHEST
MESH = pl.DeviceIdType.MESH
F32 = jnp.float32

LIB, MEAN, SHIFT, GRAM, RSZ, AGZ, RSC, AGC = range(8)

SLOT = 24
PANEL = 32


def dot(left, right, dims):
    return lax.dot_general(left, right, (dims, ((), ())), precision=HIGHEST, preferred_element_type=F32)


NN = ((1,), (0,))
NT = ((1,), (1,))
TN = ((0,), (0,))


def factor_panel(step, s_ref, w_ref):
    k = s_ref.shape[0]
    upper, lower = s_ref[0:PANEL, :], w_ref[0:PANEL, :]
    sub = lax.broadcasted_iota(jnp.int32, (PANEL, 1), 0)
    for i in range(PANEL):
        ratio = jnp.where(sub > i, upper[:, i : i + 1] / upper[i : i + 1, i : i + 1], 0.0)
        upper, lower = upper - ratio * upper[i : i + 1, :], lower - ratio * lower[i : i + 1, :]
    lane = lax.broadcasted_iota(jnp.int32, (PANEL, k), 1)
    row = lax.broadcasted_iota(jnp.int32, (PANEL, k), 0)
    pivots = jnp.sum(jnp.where(lane == row, upper, 0.0), axis=1, keepdims=True)
    scale = 1.0 / jnp.sqrt(pivots)
    upper, lower = upper * scale, lower * scale
    ahead = jnp.where((lane >= PANEL) & (lane < k - PANEL * step), upper, 0.0)
    s_new = s_ref[PANEL:k, :] - dot(ahead, upper, TN)[PANEL:k, :]
    w_new = w_ref[PANEL:k, :] - dot(ahead, lower, TN)[PANEL:k, :]
    s_ref[0 : k - PANEL, :] = pltpu.roll(s_new, k - PANEL, 1)
    s_ref[k - PANEL : k, :] = upper
    w_ref[0 : k - PANEL, :] = w_new
    w_ref[k - PANEL : k, :] = lower


def kernel(
    ng, nc, counts_ref, prior_ref, values_ref, load_ref, score_ref,
    x_ref, xt_ref, ysend, yrecv, ychunk, yfull, lsend, lrecv, msend, mrecv, dsend, drecv,
    gsend, grecv, isend, irecv, ichunk, ifull, s_ref, w_ref, send_sem, recv_sem,
):
    cell, gene = lax.axis_index("cell"), lax.axis_index("gene")
    rows, cols = counts_ref.shape
    k = prior_ref.shape[1]
    part = rows // ng
    own = cols // nc
    grow = k // nc
    total = rows * nc

    def copy(kind, src, dst, where):
        return pltpu.make_async_remote_copy(
            src_ref=src, dst_ref=dst, send_sem=send_sem.at[kind], recv_sem=recv_sem.at[kind],
            device_id=where, device_id_type=MESH,
        )

    def to_genes(kind, src, dst):
        def send(target):
            copy(kind, src(target), dst, {"gene": target}).start()

        send((gene + ng // 2) % ng)

        def both(i, carry):
            send((gene + ng // 2 + i) % ng)
            send((gene + ng // 2 - i) % ng)
            return carry

        lax.fori_loop(1, ng // 2, both, 0)

    def to_cells(kind, src, dst):
        def send(i, carry):
            target = (cell + i) % nc
            copy(kind, src(target), dst, {"cell": target}).start()
            return carry

        lax.fori_loop(1, nc, send, 0)

    def take(kind, ref):
        copy(kind, ref, ref, {"gene": (gene + 1) % ng}).wait_recv()

    def sent(kind, ref):
        copy(kind, ref, ref, {"gene": (gene + 1) % ng}).wait_send()

    barrier = pltpu.get_barrier_semaphore()

    def greet_gene(i, carry):
        pl.semaphore_signal(barrier, 1, device_id={"gene": (gene + i) % ng}, device_id_type=MESH)
        return carry

    def greet_cell(i, carry):
        pl.semaphore_signal(barrier, 1, device_id={"cell": (cell + i) % nc}, device_id_type=MESH)
        return carry

    lax.fori_loop(1, ng, greet_gene, 0)
    lax.fori_loop(1, nc, greet_cell, 0)

    counts = counts_ref[...].astype(F32)
    lsend[...] = dot(jnp.ones((8, cols), F32), counts, NT)
    prior = prior_ref[...]
    pick = lax.broadcasted_iota(jnp.int32, (ng, k), 1) == lax.broadcasted_iota(jnp.int32, (ng, k), 0) + cell * ng
    prior_rows = dot(jnp.where(pick, 1.0, 0.0) * values_ref[...], prior, NT)
    x_ref[...] = jnp.zeros_like(x_ref)
    yfull[...] = jnp.zeros_like(yfull)
    for g in range(ng):
        x_ref[g, part : part + 1, :] = prior_rows[g : g + 1, :]

    pl.semaphore_wait(barrier, ng + nc - 2)

    to_genes(LIB, lambda t: lsend.at[pl.ds(0, 1)], lrecv.at[gene, pl.ds(0, 1)])
    lrecv[gene, 0:1, :] = lsend[0:1, :]
    take(LIB, lrecv.at[pl.ds(0, ng - 1), pl.ds(0, 1)])
    library = jnp.broadcast_to(jnp.sum(lrecv[:, 0:1, :], axis=0), (8, rows))
    factor = SCALE / dot(library, jnp.full((8, 128), 0.125, F32), TN)
    means = []
    for b in range(cols // 128):
        expression = jnp.log1p(counts[:, 128 * b : 128 * (b + 1)] * factor)
        mean = jnp.mean(expression, axis=0, keepdims=True)
        means.append(mean)
        x_ref[:, 0:part, 128 * b : 128 * (b + 1)] = (expression - mean).reshape(ng, part, 128)
    local_mean = jnp.concatenate(means, axis=1)
    msend[0:1, :] = local_mean
    to_cells(MEAN, lambda t: msend.at[pl.ds(0, 1)], mrecv.at[cell, pl.ds(0, 1)])
    mrecv[cell, 0:1, :] = local_mean

    lane8 = lax.broadcasted_iota(jnp.int32, (8, k), 1)
    row8 = lax.broadcasted_iota(jnp.int32, (8, k), 0)
    gram_pick = jnp.where((lane8 == row8 + cell * grow) & (row8 < grow), 1.0, 0.0)
    iota_s = lax.broadcasted_iota(jnp.int32, (k, k), 0)
    eye = jnp.where(iota_s == lax.broadcasted_iota(jnp.int32, (k, k), 1), 1.0, 0.0)

    for step in range(ITERS + 1):
        rsz_rows = part + 1 + (grow if step > 0 else 0)
        image = prior if step == 0 else ifull[...]
        y = dot(x_ref[...].reshape(ng * SLOT, cols), image, NN)
        if step > 0:
            sent(RSZ, ysend.at[pl.ds(0, ng - 1), pl.ds(0, rsz_prev)])
        ysend[...] = y.reshape(ng, SLOT, k)
        if step > 0:
            gram_rows = dot(dot(gram_pick, image, NT), image, NN)
            for g in range(ng):
                ysend[g, part + 1 : part + 1 + grow, :] = gram_rows[0:grow, :]
        to_genes(RSZ, lambda t: ysend.at[t, pl.ds(0, rsz_rows)], yrecv.at[gene, pl.ds(0, rsz_rows)])
        yrecv[gene] = ysend[gene]
        if step == 0:
            take(MEAN, mrecv.at[pl.ds(0, nc - 1), pl.ds(0, 1)])
            delta = local_mean - jnp.sum(mrecv[:, 0:1, :], axis=0) * (1.0 / nc)
            dsend[...] = dot(jnp.broadcast_to(delta, (8, cols)), prior, NN)
            to_genes(SHIFT, lambda t: dsend.at[pl.ds(0, 1)], drecv.at[gene, pl.ds(0, 1)])
            drecv[gene, 0:1, :] = dsend[0:1, :]
            x_ref[:, 0:part, :] = x_ref[:, 0:part, :] + delta[None]
        take(RSZ, yrecv.at[pl.ds(0, ng - 1), pl.ds(0, rsz_rows)])
        chunk = jnp.sum(yrecv[...], axis=0)
        if step > 0:
            sent(AGZ, yfull.at[pl.ds(0, ng - 1), pl.ds(0, part + 1)])
        ychunk[...] = chunk
        to_genes(AGZ, lambda t: ychunk.at[pl.ds(0, part + 1)], yfull.at[gene, pl.ds(0, part + 1)])
        yfull[gene, 0 : part + 1, :] = chunk[0 : part + 1, :]
        if step > 0:
            if step > 1:
                sent(GRAM, grecv.at[pl.ds(0, nc - 1), pl.ds(0, grow)])
            gsend[0:grow, :] = chunk[part + 1 : part + 1 + grow, :]
            to_cells(GRAM, lambda t: gsend.at[pl.ds(0, grow)], grecv.at[cell, pl.ds(0, grow)])
            grecv[cell, 0:grow, :] = gsend[0:grow, :]
        else:
            lanes = lax.broadcasted_iota(jnp.int32, (1, ng * SLOT), 1)
            xt_ref[...] = x_ref[...].reshape(ng * SLOT, cols).T * jnp.where(lanes % SLOT < part, 1.0 / total, 1.0)
            take(SHIFT, drecv.at[pl.ds(0, ng - 1), pl.ds(0, 1)])
        if step == ITERS:
            take(GRAM, grecv.at[pl.ds(0, nc - 1), pl.ds(0, grow)])
            for c in range(nc):
                s_ref[c * grow : (c + 1) * grow, :] = grecv[c, 0:grow, :]
            w_ref[...] = eye
            lax.fori_loop(0, k // PANEL, lambda i, a: (factor_panel(i, s_ref, w_ref), a)[1], 0)
            inverse = w_ref[...]
            load_ref[...] = dot(image, inverse, NT) * jnp.sqrt(F32(cols * ng))
        take(AGZ, yfull.at[pl.ds(0, ng - 1), pl.ds(0, part + 1)])
        if step == ITERS:
            score_ref[...] = dot(yfull[:, 0:part, :].reshape(rows, k), inverse, NT)
            break
        if step == 0:
            yfull[:, 0:part, :] = yfull[:, 0:part, :] + jnp.sum(drecv[:, 0:1, :], axis=0)[None]
        partial = dot(xt_ref[...], yfull[...].reshape(ng * SLOT, k), NN)
        if step > 0:
            sent(RSC, irecv.at[pl.ds(0, nc - 1)])
        isend[...] = partial.reshape(nc, own, k)
        to_cells(RSC, lambda t: isend.at[t], irecv.at[cell])
        irecv[cell] = isend[cell]
        if step > 0:
            take(GRAM, grecv.at[pl.ds(0, nc - 1), pl.ds(0, grow)])
            for c in range(nc):
                s_ref[c * grow : (c + 1) * grow, :] = grecv[c, 0:grow, :]
            w_ref[...] = eye
            lax.fori_loop(0, 2, lambda i, a: (factor_panel(i, s_ref, w_ref), a)[1], 0)
        take(RSC, irecv.at[pl.ds(0, nc - 1)])
        mine = jnp.sum(irecv[...], axis=0)
        if step > 0:
            sent(AGC, ifull.at[pl.ds(0, (nc - 1) * own)])
        ichunk[...] = mine
        place = pl.ds(pl.multiple_of(cell * own, own), own)
        to_cells(AGC, lambda t: ichunk, ifull.at[place])
        ifull[place, :] = mine
        if step > 0:
            lax.fori_loop(2, k // PANEL, lambda i, a: (factor_panel(i, s_ref, w_ref), a)[1], 0)
        take(AGC, ifull.at[pl.ds(0, (nc - 1) * own)])
        if step > 0:
            ifull[...] = dot(ifull[...], w_ref[...], NT)
        rsz_prev = rsz_rows

    sent(LIB, lrecv.at[pl.ds(0, ng - 1), pl.ds(0, 1)])
    sent(MEAN, mrecv.at[pl.ds(0, nc - 1), pl.ds(0, 1)])
    sent(SHIFT, drecv.at[pl.ds(0, ng - 1), pl.ds(0, 1)])
    sent(GRAM, grecv.at[pl.ds(0, nc - 1), pl.ds(0, grow)])
    sent(RSZ, ysend.at[pl.ds(0, ng - 1), pl.ds(0, rsz_rows)])
    sent(AGZ, yfull.at[pl.ds(0, ng - 1), pl.ds(0, part + 1)])
    sent(RSC, irecv.at[pl.ds(0, nc - 1)])
    sent(AGC, ifull.at[pl.ds(0, (nc - 1) * own)])


def solution(mesh):
    ng, nc = mesh.shape["gene"], mesh.shape["cell"]

    def per_device(counts, prior_basis, prior_values):
        rows, cols = counts.shape
        k = prior_basis.shape[1]
        part, own = rows // ng, cols // nc
        vmem = pl.BlockSpec(memory_space=pltpu.VMEM)
        scratch = [
            (ng, SLOT, cols), (cols, ng * SLOT),
            (ng, SLOT, k), (ng, SLOT, k), (SLOT, k), (ng, SLOT, k),
            (8, rows), (ng, 8, rows),
            (8, cols), (nc, 8, cols),
            (8, k), (ng, 8, k),
            (8, k), (nc, 8, k),
            (nc, own, k), (nc, own, k), (own, k), (cols, k),
            (k, k), (k, k),
        ]
        return pl.pallas_call(
            functools.partial(kernel, ng, nc),
            out_shape=(jax.ShapeDtypeStruct((cols, k), F32), jax.ShapeDtypeStruct((rows, k), F32)),
            in_specs=[vmem] * 3,
            out_specs=(vmem, vmem),
            scratch_shapes=[pltpu.VMEM(s, F32) for s in scratch]
            + [pltpu.SemaphoreType.DMA((8,)), pltpu.SemaphoreType.DMA((8,))],
            compiler_params=pltpu.CompilerParams(
                collective_id=0, has_side_effects=True, vmem_limit_bytes=40 * 2**20
            ),
        )(counts, prior_basis, prior_values.reshape(1, k))

    return jax.shard_map(
        per_device,
        mesh=mesh,
        in_specs=(P("cell", "gene"), P("gene", None), P()),
        out_specs=(P("gene", None), P("cell", None)),
        check_vma=False,
    )
```

time: 1610 us -> 163 us (0.10)
  waiting for transfers between devices: 949 us -> 0 us
  blocking collectives: 234 us -> 0 us
  other arithmetic: 184 us -> 0 us
  Pallas kernels: 0 us -> 159 us
  loops' own time: 125 us -> 0 us
  local copies, waits for them, and re-layouts: 64.7 us -> 4 us
  matrix products: 25 us -> 0 us
    psum x7 -> x0, waiting for transfers between devices: 863 us -> none  [the longest x3 393 us: per_device(): lax.psum((matmul(expression, basis), inner(prior_basis, basis)), 'gene')]
    pallas_call x0 -> x1, Pallas kernels: none -> 159 us  [per_device(): pl.pallas_call(functools.partial(kernel, ng, nc), out_shape=(jax.ShapeDty...]
    another operation x3 -> x0, loops' own time: 125 us -> none  [merged_2(): return lax.fori_loop(1, lax.axis_size(axis), turn, leading)]
    all_gather x4 -> x0, blocking collectives: 119 us -> none  [merged_2(): everything = jax.tree.map(lambda part: lax.all_gather(part, axis), value)]
    add x186 -> x0, other arithmetic: 104 us -> none  [the longest x93 102 us: combine(): image_a + image_b + count_a * share * delta[:, None] * delta_proj[None, :]]
    all_gather x3 -> x0, waiting for transfers between devices: 85.9 us -> none  [merged_2(): everything = jax.tree.map(lambda part: lax.all_gather(part, axis), value)]
    another operation x15 -> x0, other arithmetic: 68.6 us -> none  [the longest x9 37.2 us: orthonormal(): lower = jnp.linalg.cholesky(lower_gram)]
    unnamed x1 -> x0, blocking collectives: 62.6 us -> none
  transfers between devices with their start and end apart: 10 -> 0, of which waited for: 9 -> 0; matrix products, arithmetic and copies ran while one was open for 0% -> 0% of each run, Pallas kernels for 0% -> 0%
where the time goes in v1:
time: 163 us
  Pallas kernels  159 us (98%)
  local copies, waits for them, and re-layouts  4 us (2%)
    pallas_call x1, Pallas kernels, per_device(): pl.pallas_call(functools.partial(kernel, ng, nc), out_shape=(jax.ShapeDty...  159 us
    unnamed x8, local copies, waits for them, and re-layouts  4 us

profile of v1, /device:TPU:1, one launch (start us, length us, event | category | flops | bytes accessed | tf_op | source)
XLA Modules:
  0.0 163.3 jit_solution(12438035101117071128)
XLA Ops:
  0.6 0.0 copy-start.2
  0.6 0.6 copy-done.2
  1.3 0.0 copy-start
  1.3 1.0 copy-done
  2.3 0.0 copy-start.1
  2.3 0.9 copy-done.1
  3.3 158.6 %shard_map.50 = (f32[512,128]{1,0:T(8,128)S(1)}, f32[256,128]{1,0:T(8,128)S(1)}) custom-call(s32[256,512]{1,0:T(8,128)S(1)} %copy-done, f32[512,128]{1,0:T(8,128)S(1)} %copy-done.1, f32[1,128]{1,0:T(1,128)S(1)} %bitcast.1), custom_call_target="tpu_custom_call" | custom-call | tf_op jit(solution)/shard_map/pallas_call | solution.py:251
  161.9 0.7 copy.7
  162.6 0.7 copy.8
Async XLA Ops:
  0.6 0.7 copy-start.2
  1.3 1.0 copy-start
  2.3 0.9 copy-start.1

commit v2 on v1

v2 whole, which is shorter than its diff:
```python
import functools

import jax
import jax.numpy as jnp
from jax import lax
from jax.experimental import pallas as pl
from jax.experimental.pallas import tpu as pltpu
from jax.sharding import PartitionSpec as P

ITERS = 3
SCALE = 10000.0
HIGHEST = lax.Precision.HIGHEST
MESH = pl.DeviceIdType.MESH
F32 = jnp.float32

LIB, MEAN, SHIFT, RSZ, AGZ, RSC, AGC, GRAM_C, GRAM_Z, GRAM = range(10)

SLOT = 24
PANEL, BLOCK = 32, 8


def dot(left, right, dims):
    return lax.dot_general(left, right, (dims, ((), ())), precision=HIGHEST, preferred_element_type=F32)


NN = ((1,), (0,))
NT = ((1,), (1,))
TN = ((0,), (0,))


def split(value):
    high = value.astype(jnp.bfloat16)
    rest = value - high.astype(F32)
    middle = rest.astype(jnp.bfloat16)
    return high, middle, (rest - middle.astype(F32)).astype(jnp.bfloat16)


def product(parts, right):
    n = right.shape[1]
    high, middle, low = split(right)
    wide = jnp.concatenate([high, middle], axis=1)

    def mxu(a, b):
        return jnp.dot(a, b, preferred_element_type=F32)

    first, second = mxu(parts[0][...], wide), mxu(parts[1][...], wide)
    small = mxu(parts[2][...], high) + mxu(parts[0][...], low) + second[:, n:]
    return first[:, :n] + (first[:, n:] + second[:, :n] + small)


def factor_panel(step, s_ref, w_ref):
    k = s_ref.shape[0]
    upper, lower = s_ref[0:PANEL, :], w_ref[0:PANEL, :]
    sub = lax.broadcasted_iota(jnp.int32, (PANEL, k), 0)
    lane = lax.broadcasted_iota(jnp.int32, (PANEL, k), 1)
    for b in range(0, PANEL, BLOCK):
        columns = [jnp.broadcast_to(upper[:, b + j : b + j + 1], (PANEL, k)) for j in range(BLOCK)]
        for j in range(BLOCK):
            i = b + j
            ratio = jnp.where(sub > i, columns[j] * (1.0 / columns[j][i : i + 1, :]), 0.0)
            for later in range(j + 1, BLOCK):
                columns[later] = columns[later] - ratio * columns[later][i : i + 1, :]
            upper = upper - ratio * upper[i : i + 1, :]
            lower = lower - ratio * lower[i : i + 1, :]
    pivots = jnp.sum(jnp.where(lane == sub, upper, 0.0), axis=1, keepdims=True)
    scale = 1.0 / jnp.sqrt(pivots)
    upper, lower = upper * scale, lower * scale
    ahead = jnp.where((lane >= PANEL) & (lane < k - PANEL * step), upper, 0.0)
    change = dot(ahead, jnp.concatenate([upper, lower], axis=1), TN)
    s_ref[0 : k - PANEL, :] = pltpu.roll(s_ref[PANEL:k, :] - change[PANEL:k, 0:k], k - PANEL, 1)
    w_new = w_ref[PANEL:k, :] - change[PANEL:k, k : 2 * k]
    s_ref[k - PANEL : k, :] = upper
    w_ref[0 : k - PANEL, :] = w_new
    w_ref[k - PANEL : k, :] = lower


def kernel(
    ng, nc, counts_hbm, prior_hbm, values_hbm, load_ref, score_ref,
    counts_ref, prior_ref, values_ref,
    x_ref, ysend, yrecv, ychunk, yfull, lsend, lrecv, msend, mrecv, dsend, drecv,
    gsend, grecv, zsend, zrecv, csend, crecv, isend, irecv, ichunk, ifull, s_ref, w_ref,
    x_high, x_middle, x_low, t_high, t_middle, t_low, send_sem, recv_sem, load_sem,
):
    cell, gene = lax.axis_index("cell"), lax.axis_index("gene")
    rows, cols = counts_ref.shape
    k = prior_ref.shape[1]
    part = rows // ng
    own = cols // nc
    grow = k // nc
    total = rows * nc
    x_parts, t_parts = (x_high, x_middle, x_low), (t_high, t_middle, t_low)

    loads = [
        pltpu.make_async_copy(src, dst, load_sem.at[i])
        for i, (src, dst) in enumerate(
            [(counts_hbm, counts_ref), (prior_hbm, prior_ref), (values_hbm, values_ref)]
        )
    ]
    for load in loads:
        load.start()

    def copy(kind, src, dst, where):
        return pltpu.make_async_remote_copy(
            src_ref=src, dst_ref=dst, send_sem=send_sem.at[kind], recv_sem=recv_sem.at[kind],
            device_id=where, device_id_type=MESH,
        )

    def to_genes(kind, src, dst):
        def send(target):
            copy(kind, src(target), dst, {"gene": target}).start()

        send(lax.rem(gene + ng // 2, ng))

        def both(i, carry):
            send(lax.rem(gene + ng // 2 + i, ng))
            send(lax.rem(gene + ng // 2 - i + ng, ng))
            return carry

        lax.fori_loop(1, ng // 2, both, 0)

    core = lax.rem(cell, 2)
    chip_y = lax.rem(lax.div(cell, 2), 4)
    chip_x = lax.div(cell, 8)

    def turn(i):
        half = lax.div(i, 2)
        return lax.rem(2 + 3 * i + half * (3 + 2 * lax.rem(i, 2)), 4)

    def to_cells(kind, src, dst):
        def send(i, carry):
            x = lax.rem(chip_x + turn(lax.div(i, 8)), 4)
            y = lax.rem(chip_y + turn(lax.rem(lax.div(i, 2), 4)), 4)
            target = x * 8 + y * 2 + lax.rem(core + 1 + i, 2)
            copy(kind, src(target), dst, {"cell": target}).start()
            return carry

        lax.fori_loop(0, nc - 1, send, 0)

    def take(kind, ref):
        copy(kind, ref, ref, {"gene": lax.rem(gene + 1, ng)}).wait_recv()

    def sent(kind, ref):
        copy(kind, ref, ref, {"gene": lax.rem(gene + 1, ng)}).wait_send()

    weight = {
        LIB: lrecv.at[pl.ds(0, ng - 1), pl.ds(0, 1)],
        MEAN: mrecv.at[pl.ds(0, nc - 1), pl.ds(0, 1)],
        SHIFT: drecv.at[pl.ds(0, ng - 1), pl.ds(0, 1)],
        RSZ: yrecv.at[pl.ds(0, ng - 1), pl.ds(0, part + 1)],
        AGZ: yfull.at[pl.ds(0, ng - 1), pl.ds(0, part + 1)],
        RSC: irecv.at[pl.ds(0, nc - 1)],
        AGC: ifull.at[pl.ds(0, (nc - 1) * own)],
        GRAM_C: grecv.at[pl.ds(0, nc - 1)],
        GRAM_Z: zrecv.at[pl.ds(0, ng - 1)],
        GRAM: crecv.at[pl.ds(0, nc - 1)],
    }

    barrier = pltpu.get_barrier_semaphore()

    def greet_gene(i, carry):
        pl.semaphore_signal(barrier, 1, device_id={"gene": lax.rem(gene + i, ng)}, device_id_type=MESH)
        return carry

    def greet_cell(i, carry):
        pl.semaphore_signal(barrier, 1, device_id={"cell": lax.rem(cell + i, nc)}, device_id_type=MESH)
        return carry

    lax.fori_loop(1, ng, greet_gene, 0)
    lax.fori_loop(1, nc, greet_cell, 0)

    loads[0].wait()
    counts = counts_ref[...].astype(F32)
    lsend[...] = lax.dot_general(
        jnp.ones((8, cols), jnp.bfloat16), counts.astype(jnp.bfloat16), (NT, ((), ())), preferred_element_type=F32
    )
    loads[1].wait()
    loads[2].wait()
    prior = prior_ref[...]
    pick = lax.broadcasted_iota(jnp.int32, (ng, k), 1) == lax.broadcasted_iota(jnp.int32, (ng, k), 0) + cell * ng
    prior_rows = dot(jnp.where(pick, 1.0, 0.0) * values_ref[...], prior, NT)
    x_ref[...] = jnp.zeros_like(x_ref)
    yfull[...] = jnp.zeros_like(yfull)
    for g in range(ng):
        x_ref[g, part : part + 1, :] = prior_rows[g : g + 1, :]

    pl.semaphore_wait(barrier, ng + nc - 2)

    to_genes(LIB, lambda t: lsend.at[pl.ds(0, 1)], lrecv.at[gene, pl.ds(0, 1)])
    lrecv[gene, 0:1, :] = lsend[0:1, :]
    take(LIB, weight[LIB])
    library = jnp.broadcast_to(jnp.sum(lrecv[:, 0:1, :], axis=0), (8, rows))
    factor = SCALE / dot(library, jnp.full((8, 128), 0.125, F32), TN)
    means = []
    for b in range(cols // 128):
        expression = jnp.log1p(counts_ref[:, 128 * b : 128 * (b + 1)].astype(F32) * factor)
        mean = jnp.mean(expression, axis=0, keepdims=True)
        means.append(mean)
        x_ref[:, 0:part, 128 * b : 128 * (b + 1)] = (expression - mean).reshape(ng, part, 128)
    local_mean = jnp.concatenate(means, axis=1)
    msend[0:1, :] = local_mean
    to_cells(MEAN, lambda t: msend.at[pl.ds(0, 1)], mrecv.at[cell, pl.ds(0, 1)])
    mrecv[cell, 0:1, :] = local_mean

    place = pl.ds(pl.multiple_of(cell * own, own), own)

    def scatter_genes(y):
        ysend[...] = y.reshape(ng, SLOT, k)
        to_genes(RSZ, lambda t: ysend.at[t, pl.ds(0, part + 1)], yrecv.at[gene, pl.ds(0, part + 1)])
        yrecv[gene] = ysend[gene]

    def gather_genes():
        take(RSZ, weight[RSZ])
        ychunk[...] = jnp.sum(yrecv[...], axis=0)
        to_genes(AGZ, lambda t: ychunk.at[pl.ds(0, part + 1)], yfull.at[gene, pl.ds(0, part + 1)])
        yfull[gene, 0 : part + 1, :] = ychunk[0 : part + 1, :]

    def scatter_cells():
        isend[...] = product(t_parts, yfull[...].reshape(ng * SLOT, k)).reshape(nc, own, k)
        to_cells(RSC, lambda t: isend.at[t], irecv.at[cell])
        irecv[cell] = isend[cell]

    def gather_cells(mine):
        ichunk[...] = mine
        to_cells(AGC, lambda t: ichunk, ifull.at[place])
        ifull[place, :] = mine
        gram = dot(mine, mine, TN)
        for c in range(nc):
            gsend[c] = gram[c * grow : (c + 1) * grow, :]
        to_cells(GRAM_C, lambda t: gsend.at[t], grecv.at[cell])
        grecv[cell] = gsend[cell]

    def gram_genes():
        take(GRAM_C, weight[GRAM_C])
        zsend[...] = jnp.sum(grecv[...], axis=0)
        to_genes(GRAM_Z, lambda t: zsend, zrecv.at[gene])
        zrecv[gene] = zsend[...]

    def gram_cells():
        take(GRAM_Z, weight[GRAM_Z])
        csend[...] = jnp.sum(zrecv[...], axis=0)
        to_cells(GRAM, lambda t: csend, crecv.at[cell])
        crecv[cell] = csend[...]

    def factorise():
        take(GRAM, weight[GRAM])
        for c in range(nc):
            s_ref[c * grow : (c + 1) * grow, :] = crecv[c]
        w_ref[...] = jnp.where(
            lax.broadcasted_iota(jnp.int32, (k, k), 0) == lax.broadcasted_iota(jnp.int32, (k, k), 1), 1.0, 0.0
        )

        def panel(i, carry):
            factor_panel(i, s_ref, w_ref)
            return carry

        lax.fori_loop(0, k // PANEL, panel, 0)

    scatter_genes(dot(x_ref[...].reshape(ng * SLOT, cols), prior, NN))
    take(MEAN, weight[MEAN])
    delta = local_mean - jnp.sum(mrecv[:, 0:1, :], axis=0) * (1.0 / nc)
    dsend[...] = dot(jnp.broadcast_to(delta, (8, cols)), prior, NN)
    to_genes(SHIFT, lambda t: dsend.at[pl.ds(0, 1)], drecv.at[gene, pl.ds(0, 1)])
    drecv[gene, 0:1, :] = dsend[0:1, :]
    x_ref[:, 0:part, :] = x_ref[:, 0:part, :] + delta[None]
    gather_genes()
    x = x_ref[...].reshape(ng * SLOT, cols)
    for ref, value in zip(x_parts, split(x)):
        ref[...] = value
    lanes = lax.broadcasted_iota(jnp.int32, (1, ng * SLOT), 1)
    for ref, value in zip(t_parts, split(x.T * jnp.where(lanes % SLOT < part, 1.0 / total, 1.0))):
        ref[...] = value
    take(SHIFT, weight[SHIFT])
    take(AGZ, weight[AGZ])
    yfull[:, 0:part, :] = yfull[:, 0:part, :] + jnp.sum(drecv[:, 0:1, :], axis=0)[None]
    scatter_cells()
    sent(RSZ, weight[RSZ])
    sent(AGZ, weight[AGZ])
    take(RSC, weight[RSC])
    gather_cells(jnp.sum(irecv[...], axis=0))

    def to_basis():
        gram_genes()
        take(AGC, weight[AGC])
        scatter_genes(product(x_parts, ifull[...]))
        gram_cells()
        gather_genes()
        factorise()

    def iteration(step, carry):
        to_basis()
        take(AGZ, weight[AGZ])
        sent(RSC, weight[RSC])
        scatter_cells()
        for kind in (RSZ, AGZ, AGC, GRAM_C, GRAM_Z, GRAM):
            sent(kind, weight[kind])
        take(RSC, weight[RSC])
        gather_cells(dot(jnp.sum(irecv[...], axis=0), w_ref[...], NT))
        return carry

    lax.fori_loop(1, ITERS, iteration, 0)

    to_basis()
    load_ref[...] = dot(ifull[...], w_ref[...], NT) * jnp.sqrt(F32(cols * ng))
    take(AGZ, weight[AGZ])
    score_ref[...] = dot(yfull[:, 0:part, :].reshape(rows, k), w_ref[...], NT)
    for kind in (LIB, MEAN, SHIFT, RSC, RSZ, AGZ, AGC, GRAM_C, GRAM_Z, GRAM):
        sent(kind, weight[kind])


def solution(mesh):
    ng, nc = mesh.shape["gene"], mesh.shape["cell"]

    def per_device(counts, prior_basis, prior_values):
        rows, cols = counts.shape
        k = prior_basis.shape[1]
        part, own = rows // ng, cols // nc
        grow = k // nc
        vmem, hbm = pl.BlockSpec(memory_space=pltpu.VMEM), pl.BlockSpec(memory_space=pltpu.HBM)
        scratch = [
            (cols, k), (1, k),
            (ng, SLOT, cols),
            (ng, SLOT, k), (ng, SLOT, k), (SLOT, k), (ng, SLOT, k),
            (8, rows), (ng, 8, rows),
            (8, cols), (nc, 8, cols),
            (8, k), (ng, 8, k),
            (nc, grow, k), (nc, grow, k), (grow, k), (ng, grow, k), (grow, k), (nc, grow, k),
            (nc, own, k), (nc, own, k), (own, k), (cols, k),
            (k, k), (k, k),
        ]
        return pl.pallas_call(
            functools.partial(kernel, ng, nc),
            out_shape=(jax.ShapeDtypeStruct((cols, k), F32), jax.ShapeDtypeStruct((rows, k), F32)),
            in_specs=[hbm] * 3,
            out_specs=(vmem, vmem),
            scratch_shapes=[pltpu.VMEM((rows, cols), jnp.int32)]
            + [pltpu.VMEM(s, F32) for s in scratch]
            + [pltpu.VMEM((ng * SLOT, cols), jnp.bfloat16)] * 3
            + [pltpu.VMEM((cols, ng * SLOT), jnp.bfloat16)] * 3
            + [pltpu.SemaphoreType.DMA((10,)), pltpu.SemaphoreType.DMA((10,)), pltpu.SemaphoreType.DMA((3,))],
            compiler_params=pltpu.CompilerParams(
                collective_id=0, has_side_effects=True, vmem_limit_bytes=56_000_000
            ),
        )(counts, prior_basis, prior_values.reshape(1, k))

    return jax.shard_map(
        per_device,
        mesh=mesh,
        in_specs=(P("cell", "gene"), P("gene", None), P()),
        out_specs=(P("gene", None), P("cell", None)),
        check_vma=False,
    )
```

time: 163 us -> 144 us (0.88)
  Pallas kernels: 159 us -> 140 us
  local copies, waits for them, and re-layouts: 4 us -> 2.01 us
    pallas_call x1, Pallas kernels: 159 us -> 140 us  [per_device(): pl.pallas_call(functools.partial(kernel, ng, nc), out_shape=(jax.ShapeDty...]
    unnamed x8 -> x4, local copies, waits for them, and re-layouts: 4 us -> 2.01 us
where the time goes in v2:
time: 144 us; the launch traced here: 143 us
  Pallas kernels  140 us (97%)
  local copies, waits for them, and re-layouts  2.01 us (1%)
    pallas_call x1, Pallas kernels, per_device(): pl.pallas_call(functools.partial(kernel, ng, nc), out_shape=(jax.ShapeDty...  140 us

profile of v2, /device:TPU:1, one launch (start us, length us, event | category | flops | bytes accessed | tf_op | source)
XLA Modules:
  0.0 143.0 jit_solution(10690420876962174313)
XLA Ops:
  0.6 0.0 copy-start
  0.6 0.6 copy-done
  1.3 140.3 %shard_map.50 = (f32[512,128]{1,0:T(8,128)S(1)}, f32[256,128]{1,0:T(8,128)S(1)}) custom-call(s32[256,512]{1,0:T(8,128)} %counts_hbm.1, f32[512,128]{1,0:T(8,128)} %prior_hbm.1, f32[1,128]{1,0:T(1,128)S(1)} %bitcast.1), custom_call_target="tpu_custom_call" | custom-call | tf_op jit(solution)/shard_map/pallas_call | solution.py:330
  141.6 0.7 copy.7
  142.3 0.7 copy.8
Async XLA Ops:
  0.6 0.7 copy-start

commit v3 on v2

--- a/solution.py
+++ b/solution.py
@@ -13,7 +13,8 @@
 MESH = pl.DeviceIdType.MESH
 F32 = jnp.float32
 
-LIB, MEAN, SHIFT, RSZ, AGZ, RSC, AGC, GRAM_C, GRAM_Z, GRAM = range(10)
+KINDS = 11
+LIB, MEAN, SHIFT, RSZ, AGZ, RSC, AGC, GRAM_C, GRAM, GRAM_Z, _ = range(KINDS)
 
 SLOT = 24
 PANEL, BLOCK = 32, 8
@@ -48,7 +49,7 @@
     return first[:, :n] + (first[:, n:] + second[:, :n] + small)
 
 
-def factor_panel(step, s_ref, w_ref):
+def factor_panel(step, s_ref, w_ref, last=False):
     k = s_ref.shape[0]
     upper, lower = s_ref[0:PANEL, :], w_ref[0:PANEL, :]
     sub = lax.broadcasted_iota(jnp.int32, (PANEL, k), 0)
@@ -65,6 +66,10 @@
     pivots = jnp.sum(jnp.where(lane == sub, upper, 0.0), axis=1, keepdims=True)
     scale = 1.0 / jnp.sqrt(pivots)
     upper, lower = upper * scale, lower * scale
+    if last:
+        w_ref[0 : k - PANEL, :] = w_ref[PANEL:k, :]
+        w_ref[k - PANEL : k, :] = lower
+        return
     ahead = jnp.where((lane >= PANEL) & (lane < k - PANEL * step), upper, 0.0)
     change = dot(ahead, jnp.concatenate([upper, lower], axis=1), TN)
     s_ref[0 : k - PANEL, :] = pltpu.roll(s_ref[PANEL:k, :] - change[PANEL:k, 0:k], k - PANEL, 1)
@@ -105,18 +110,15 @@
             device_id=where, device_id_type=MESH,
         )
 
-    def to_genes(kind, src, dst):
-        def send(target):
-            copy(kind, src(target), dst, {"gene": target}).start()
-
-        send(lax.rem(gene + ng // 2, ng))
+    def genes(act):
+        act(lax.rem(gene + ng // 2, ng))
 
         def both(i, carry):
-            send(lax.rem(gene + ng // 2 + i, ng))
-            send(lax.rem(gene + ng // 2 - i + ng, ng))
+            act(lax.rem(gene + ng // 2 + i, ng))
+            act(lax.rem(gene + ng // 2 - i + ng, ng))
             return carry
 
-        lax.fori_loop(1, ng // 2, both, 0)
+        lax.fori_loop(1, ng // 2, both, 0, unroll=True)
 
     core = lax.rem(cell, 2)
     chip_y = lax.rem(lax.div(cell, 2), 4)
@@ -126,15 +128,20 @@
         half = lax.div(i, 2)
         return lax.rem(2 + 3 * i + half * (3 + 2 * lax.rem(i, 2)), 4)
 
-    def to_cells(kind, src, dst):
-        def send(i, carry):
+    def cells(act):
+        def one(i, carry):
             x = lax.rem(chip_x + turn(lax.div(i, 8)), 4)
             y = lax.rem(chip_y + turn(lax.rem(lax.div(i, 2), 4)), 4)
-            target = x * 8 + y * 2 + lax.rem(core + 1 + i, 2)
-            copy(kind, src(target), dst, {"cell": target}).start()
+            act(x * 8 + y * 2 + lax.rem(core + 1 + i, 2))
             return carry
 
-        lax.fori_loop(0, nc - 1, send, 0)
+        lax.fori_loop(0, nc - 1, one, 0, unroll=True)
+
+    def to_genes(kind, src, dst):
+        genes(lambda target: copy(kind, src(target), dst, {"gene": target}).start())
+
+    def to_cells(kind, src, dst):
+        cells(lambda target: copy(kind, src(target), dst, {"cell": target}).start())
 
     def take(kind, ref):
         copy(kind, ref, ref, {"gene": lax.rem(gene + 1, ng)}).wait_recv()
@@ -146,27 +153,16 @@
         LIB: lrecv.at[pl.ds(0, ng - 1), pl.ds(0, 1)],
         MEAN: mrecv.at[pl.ds(0, nc - 1), pl.ds(0, 1)],
         SHIFT: drecv.at[pl.ds(0, ng - 1), pl.ds(0, 1)],
-        RSZ: yrecv.at[pl.ds(0, ng - 1), pl.ds(0, part + 1)],
-        AGZ: yfull.at[pl.ds(0, ng - 1), pl.ds(0, part + 1)],
         RSC: irecv.at[pl.ds(0, nc - 1)],
         AGC: ifull.at[pl.ds(0, (nc - 1) * own)],
         GRAM_C: grecv.at[pl.ds(0, nc - 1)],
-        GRAM_Z: zrecv.at[pl.ds(0, ng - 1)],
         GRAM: crecv.at[pl.ds(0, nc - 1)],
     }
 
     barrier = pltpu.get_barrier_semaphore()
 
-    def greet_gene(i, carry):
-        pl.semaphore_signal(barrier, 1, device_id={"gene": lax.rem(gene + i, ng)}, device_id_type=MESH)
-        return carry
-
-    def greet_cell(i, carry):
-        pl.semaphore_signal(barrier, 1, device_id={"cell": lax.rem(cell + i, nc)}, device_id_type=MESH)
-        return carry
-
-    lax.fori_loop(1, ng, greet_gene, 0)
-    lax.fori_loop(1, nc, greet_cell, 0)
+    genes(lambda t: pl.semaphore_signal(barrier, 1, device_id={"gene": t}, device_id_type=MESH))
+    cells(lambda t: pl.semaphore_signal(barrier, 1, device_id={"cell": t}, device_id_type=MESH))
 
     loads[0].wait()
     counts = counts_ref[...].astype(F32)
@@ -203,16 +199,22 @@
 
     place = pl.ds(pl.multiple_of(cell * own, own), own)
 
-    def scatter_genes(y):
-        ysend[...] = y.reshape(ng, SLOT, k)
-        to_genes(RSZ, lambda t: ysend.at[t, pl.ds(0, part + 1)], yrecv.at[gene, pl.ds(0, part + 1)])
+    def scatter_genes(n):
+        to_genes(RSZ, lambda t: ysend.at[t, pl.ds(0, n)], yrecv.at[gene, pl.ds(0, n)])
         yrecv[gene] = ysend[gene]
 
-    def gather_genes():
-        take(RSZ, weight[RSZ])
-        ychunk[...] = jnp.sum(yrecv[...], axis=0)
-        to_genes(AGZ, lambda t: ychunk.at[pl.ds(0, part + 1)], yfull.at[gene, pl.ds(0, part + 1)])
-        yfull[gene, 0 : part + 1, :] = ychunk[0 : part + 1, :]
+    def gather_genes(n):
+        take(RSZ, yrecv.at[pl.ds(0, ng - 1), pl.ds(0, n)])
+        ychunk[0:n, :] = jnp.sum(yrecv[:, 0:n, :], axis=0)
+        to_genes(AGZ, lambda t: ychunk.at[pl.ds(0, n)], yfull.at[gene, pl.ds(0, n)])
+        yfull[gene, 0:n, :] = ychunk[0:n, :]
+
+    def take_genes(n):
+        take(AGZ, yfull.at[pl.ds(0, ng - 1), pl.ds(0, n)])
+
+    def sent_genes(n):
+        sent(RSZ, yrecv.at[pl.ds(0, ng - 1), pl.ds(0, n)])
+        sent(AGZ, yfull.at[pl.ds(0, ng - 1), pl.ds(0, n)])
 
     def scatter_cells():
         isend[...] = product(t_parts, yfull[...].reshape(ng * SLOT, k)).reshape(nc, own, k)
@@ -229,15 +231,15 @@
         to_cells(GRAM_C, lambda t: gsend.at[t], grecv.at[cell])
         grecv[cell] = gsend[cell]
 
-    def gram_genes():
+    def gram_genes(turn):
         take(GRAM_C, weight[GRAM_C])
         zsend[...] = jnp.sum(grecv[...], axis=0)
-        to_genes(GRAM_Z, lambda t: zsend, zrecv.at[gene])
-        zrecv[gene] = zsend[...]
-
-    def gram_cells():
-        take(GRAM_Z, weight[GRAM_Z])
-        csend[...] = jnp.sum(zrecv[...], axis=0)
+        to_genes(GRAM_Z + turn, lambda t: zsend, zrecv.at[turn, gene])
+        zrecv[turn, gene] = zsend[...]
+
+    def gram_cells(turn):
+        take(GRAM_Z + turn, zrecv.at[turn, pl.ds(0, ng - 1)])
+        csend[...] = jnp.sum(zrecv[turn], axis=0)
         to_cells(GRAM, lambda t: csend, crecv.at[cell])
         crecv[cell] = csend[...]
 
@@ -253,16 +255,18 @@
             factor_panel(i, s_ref, w_ref)
             return carry
 
-        lax.fori_loop(0, k // PANEL, panel, 0)
-
-    scatter_genes(dot(x_ref[...].reshape(ng * SLOT, cols), prior, NN))
+        lax.fori_loop(0, k // PANEL - 1, panel, 0)
+        factor_panel(k // PANEL - 1, s_ref, w_ref, last=True)
+
+    ysend[...] = dot(x_ref[...].reshape(ng * SLOT, cols), prior, NN).reshape(ng, SLOT, k)
+    scatter_genes(part + 1)
     take(MEAN, weight[MEAN])
     delta = local_mean - jnp.sum(mrecv[:, 0:1, :], axis=0) * (1.0 / nc)
     dsend[...] = dot(jnp.broadcast_to(delta, (8, cols)), prior, NN)
     to_genes(SHIFT, lambda t: dsend.at[pl.ds(0, 1)], drecv.at[gene, pl.ds(0, 1)])
     drecv[gene, 0:1, :] = dsend[0:1, :]
     x_ref[:, 0:part, :] = x_ref[:, 0:part, :] + delta[None]
-    gather_genes()
+    gather_genes(part + 1)
     x = x_ref[...].reshape(ng * SLOT, cols)
     for ref, value in zip(x_parts, split(x)):
         ref[...] = value
@@ -270,40 +274,51 @@
     for ref, value in zip(t_parts, split(x.T * jnp.where(lanes % SLOT < part, 1.0 / total, 1.0))):
         ref[...] = value
     take(SHIFT, weight[SHIFT])
-    take(AGZ, weight[AGZ])
+    take_genes(part + 1)
     yfull[:, 0:part, :] = yfull[:, 0:part, :] + jnp.sum(drecv[:, 0:1, :], axis=0)[None]
     scatter_cells()
-    sent(RSZ, weight[RSZ])
-    sent(AGZ, weight[AGZ])
+    sent_genes(part + 1)
     take(RSC, weight[RSC])
     gather_cells(jnp.sum(irecv[...], axis=0))
 
-    def to_basis():
-        gram_genes()
+    def to_products():
         take(AGC, weight[AGC])
-        scatter_genes(product(x_parts, ifull[...]))
-        gram_cells()
-        gather_genes()
-        factorise()
+        ysend[...] = product(x_parts, ifull[...]).reshape(ng, SLOT, k)
 
     def iteration(step, carry):
-        to_basis()
-        take(AGZ, weight[AGZ])
+        side = lax.rem(step, 2)
+        to_products()
+        scatter_genes(part + 1)
+        gram_genes(side)
+        gather_genes(part + 1)
+        gram_cells(side)
+        take_genes(part + 1)
         sent(RSC, weight[RSC])
         scatter_cells()
-        for kind in (RSZ, AGZ, AGC, GRAM_C, GRAM_Z, GRAM):
+        factorise()
+        sent_genes(part + 1)
+        for kind in (AGC, GRAM_C, GRAM):
             sent(kind, weight[kind])
+        sent(GRAM_Z + side, zrecv.at[side, pl.ds(0, ng - 1)])
         take(RSC, weight[RSC])
         gather_cells(dot(jnp.sum(irecv[...], axis=0), w_ref[...], NT))
         return carry
 
     lax.fori_loop(1, ITERS, iteration, 0)
 
-    to_basis()
+    to_products()
+    last = ITERS % 2
+    gram_genes(last)
+    scatter_genes(part)
+    gram_cells(last)
+    gather_genes(part)
+    factorise()
     load_ref[...] = dot(ifull[...], w_ref[...], NT) * jnp.sqrt(F32(cols * ng))
-    take(AGZ, weight[AGZ])
+    take_genes(part)
     score_ref[...] = dot(yfull[:, 0:part, :].reshape(rows, k), w_ref[...], NT)
-    for kind in (LIB, MEAN, SHIFT, RSC, RSZ, AGZ, AGC, GRAM_C, GRAM_Z, GRAM):
+    sent_genes(part)
+    sent(GRAM_Z + last, zrecv.at[last, pl.ds(0, ng - 1)])
+    for kind in (LIB, MEAN, SHIFT, RSC, AGC, GRAM_C, GRAM):
         sent(kind, weight[kind])
 
 
@@ -323,7 +338,7 @@
             (8, rows), (ng, 8, rows),
             (8, cols), (nc, 8, cols),
             (8, k), (ng, 8, k),
-            (nc, grow, k), (nc, grow, k), (grow, k), (ng, grow, k), (grow, k), (nc, grow, k),
+            (nc, grow, k), (nc, grow, k), (grow, k), (2, ng, grow, k), (grow, k), (nc, grow, k),
             (nc, own, k), (nc, own, k), (own, k), (cols, k),
             (k, k), (k, k),
         ]
@@ -336,7 +351,7 @@
             + [pltpu.VMEM(s, F32) for s in scratch]
             + [pltpu.VMEM((ng * SLOT, cols), jnp.bfloat16)] * 3
             + [pltpu.VMEM((cols, ng * SLOT), jnp.bfloat16)] * 3
-            + [pltpu.SemaphoreType.DMA((10,)), pltpu.SemaphoreType.DMA((10,)), pltpu.SemaphoreType.DMA((3,))],
+            + [pltpu.SemaphoreType.DMA((KINDS,)), pltpu.SemaphoreType.DMA((KINDS,)), pltpu.SemaphoreType.DMA((3,))],
             compiler_params=pltpu.CompilerParams(
                 collective_id=0, has_side_effects=True, vmem_limit_bytes=56_000_000
             ),

time: 144 us -> 139 us (0.965)
  Pallas kernels: 140 us -> 137 us
    pallas_call x1, Pallas kernels: 140 us -> 137 us  [per_device(): pl.pallas_call(functools.partial(kernel, ng, nc), out_shape=(jax.ShapeDty...]
where the time goes in v3:
time: 139 us
  Pallas kernels  137 us (99%)
  local copies, waits for them, and re-layouts  2.01 us (1%)
    pallas_call x1, Pallas kernels, per_device(): pl.pallas_call(functools.partial(kernel, ng, nc), out_shape=(jax.ShapeDty...  137 us

profile of v3, /device:TPU:1, one launch (start us, length us, event | category | flops | bytes accessed | tf_op | source)
XLA Modules:
  0.0 139.2 jit_solution(2691379969326175271)
XLA Ops:
  0.6 0.0 copy-start
  0.6 0.6 copy-done
  1.3 136.5 %shard_map.50 = (f32[512,128]{1,0:T(8,128)S(1)}, f32[256,128]{1,0:T(8,128)S(1)}) custom-call(s32[256,512]{1,0:T(8,128)} %counts_hbm.1, f32[512,128]{1,0:T(8,128)} %prior_hbm.1, f32[1,128]{1,0:T(1,128)S(1)} %bitcast.1), custom_call_target="tpu_custom_call" | custom-call | tf_op jit(solution)/shard_map/pallas_call | solution.py:345
  137.8 0.7 copy.7
  138.5 0.7 copy.8
Async XLA Ops:
  0.6 0.7 copy-start

commit v4 on v3

--- a/solution.py
+++ b/solution.py
@@ -194,8 +194,6 @@
         x_ref[:, 0:part, 128 * b : 128 * (b + 1)] = (expression - mean).reshape(ng, part, 128)
     local_mean = jnp.concatenate(means, axis=1)
     msend[0:1, :] = local_mean
-    to_cells(MEAN, lambda t: msend.at[pl.ds(0, 1)], mrecv.at[cell, pl.ds(0, 1)])
-    mrecv[cell, 0:1, :] = local_mean
 
     place = pl.ds(pl.multiple_of(cell * own, own), own)
 
@@ -260,6 +258,8 @@
 
     ysend[...] = dot(x_ref[...].reshape(ng * SLOT, cols), prior, NN).reshape(ng, SLOT, k)
     scatter_genes(part + 1)
+    to_cells(MEAN, lambda t: msend.at[pl.ds(0, 1)], mrecv.at[cell, pl.ds(0, 1)])
+    mrecv[cell, 0:1, :] = local_mean
     take(MEAN, weight[MEAN])
     delta = local_mean - jnp.sum(mrecv[:, 0:1, :], axis=0) * (1.0 / nc)
     dsend[...] = dot(jnp.broadcast_to(delta, (8, cols)), prior, NN)

time: 139 us -> 139 us (level)
  no operation moved by 1% of the time
where the time goes in v4:
time: 139 us
  Pallas kernels  136 us (98%)
  local copies, waits for them, and re-layouts  2.01 us (1%)
    pallas_call x1, Pallas kernels, per_device(): pl.pallas_call(functools.partial(kernel, ng, nc), out_shape=(jax.ShapeDty...  136 us

profile of v4, /device:TPU:1, one launch (start us, length us, event | category | flops | bytes accessed | tf_op | source)
XLA Modules:
  0.0 139.0 jit_solution(933814807463388925)
XLA Ops:
  0.6 0.0 copy-start
  0.6 0.6 copy-done
  1.3 136.4 %shard_map.50 = (f32[512,128]{1,0:T(8,128)S(1)}, f32[256,128]{1,0:T(8,128)S(1)}) custom-call(s32[256,512]{1,0:T(8,128)} %counts_hbm.1, f32[512,128]{1,0:T(8,128)} %prior_hbm.1, f32[1,128]{1,0:T(1,128)S(1)} %bitcast.1), custom_call_target="tpu_custom_call" | custom-call | tf_op jit(solution)/shard_map/pallas_call | solution.py:345
  137.7 0.7 copy.7
  138.4 0.7 copy.8
Async XLA Ops:
  0.6 0.7 copy-start
